TPU v7x, 32 devices: a whole 2x2x4 slice. The times are simulated.
32 devices in a mesh: groups: 2 (over y), row: 4 (over z), col: 4 (over x, core).
Axes of the slice: x: 2, y: 2, z: 4, core: 2. Of those that a mesh axis runs over, the one named last changes fastest.
Arguments:
- base_density: bfloat16 [8, 8, 9, 184, 184], P(('groups', 'row'), 'col'), parts along dimension 0, as said below
- tangent_density: bfloat16 [8, 8, 9, 184, 184], P(('groups', 'row'), 'col'), parts along dimension 0, as said below
- pattern: int32 [4, 8, 9, 8, 8], P('row', 'col'), may hold values from 0 to 1, as said below
Outputs:
- tangent_step: bfloat16 [8, 8, 9, 184, 184], P(('groups', 'row'), 'col'), parts along dimension 0
There are 2 independent parts, one for each index of `groups`. A program takes and returns all parts, laid end to end along the dimension named above; an argument that names none is the same for every part. Nothing has to cross between parts.
Inputs may be any that keep to these rules, and one draw needn't show every extreme that they name: pattern is symmetric: pattern[x, y, o, z, z'] equals pattern[(x + sx) mod 4, (y + sy) mod 8, 8 - o, z', z]; the blocks on the diagonal (o = 4, z = z') are kept. base_density is a symmetric matrix in the layout of the steps. tangent_density is a symmetric matrix in the layout of the steps.
All inputs are finite; a program needn't handle non-finite values.
Results may differ from a plain program's by a relative error of at most 0.0068.
Values may be sent and summed in bfloat16 or wider, within the bound.
A program may use at most 128 MiB of HBM per device.

v0:
```python
import jax
import jax.numpy as jnp
from jax import lax
from jax.sharding import PartitionSpec as P

BLOCK = 23


def with_halo(block, sides, width):
    for axis, dim in sides:
        count = lax.axis_size(axis)
        forward = [(i, i + 1) for i in range(count - 1)]
        forward.append((count - 1, 0))
        backward = [(target, source) for source, target in forward]
        low = lax.ppermute(
            lax.slice_in_dim(block, block.shape[dim] - width, None, axis=dim), axis, forward
        )
        high = lax.ppermute(lax.slice_in_dim(block, 0, width, axis=dim), axis, backward)
        block = jnp.concatenate([low, block, high], axis=dim)
    return block


def expand(pattern):
    wide = jnp.repeat(jnp.repeat(pattern, BLOCK, axis=-2), BLOCK, axis=-1)
    return wide.astype(jnp.float32)


def shifts(offset):
    return (offset // 3 - 1, offset % 3 - 1)


def joined(first_off, second_off):
    first_x, first_y = shifts(first_off)
    second_x, second_y = shifts(second_off)
    total_x = first_x + second_x
    total_y = first_y + second_y
    if abs(total_x) > 1 or abs(total_y) > 1:
        return -1
    return (total_x + 1) * 3 + total_y + 1


def neighbour_tiles(padded, offset, width_x, width_y):
    shift_x, shift_y = shifts(offset)
    return padded[1 + shift_x : 1 + shift_x + width_x, 1 + shift_y : 1 + shift_y + width_y]


def tile_product(left, padded):
    width_x, width_y = (left.shape[0], left.shape[1])
    totals = [None] * 9
    for first_off in range(9):
        moved = neighbour_tiles(padded, first_off, width_x, width_y)
        left_tile = left[:, :, first_off]
        for second_off in range(9):
            target = joined(first_off, second_off)
            if target < 0:
                continue
            term = jnp.einsum(
                "xyab,xybc->xyac",
                left_tile,
                moved[:, :, second_off],
                preferred_element_type=jnp.float32,
            )
            totals[target] = term if totals[target] is None else totals[target] + term
    return jnp.stack(totals, axis=2)


def shards(base_density, tangent_density, pattern):
    block_mask = expand(pattern)
    base_kept = (base_density.astype(jnp.float32) * block_mask).astype(jnp.bfloat16)
    tangent_kept = (tangent_density.astype(jnp.float32) * block_mask).astype(jnp.bfloat16)
    tangent_padded = with_halo(tangent_kept, (("row", 0), ("col", 1)), 1)
    first_term = block_mask * tile_product(base_kept, tangent_padded)
    base_padded = with_halo(base_kept, (("row", 0), ("col", 1)), 1)
    second_term = block_mask * tile_product(tangent_kept, base_padded)
    first_round = first_term.astype(jnp.bfloat16)
    summed = (first_term + second_term).astype(jnp.bfloat16)
    round_padded = with_halo(first_round, (("row", 0), ("col", 1)), 1)
    third_term = block_mask * tile_product(base_kept, round_padded)
    fourth_term = block_mask * tile_product(summed, base_padded)
    result = 3.0 * (first_term + second_term) - 2.0 * (third_term + fourth_term)
    return result.astype(jnp.bfloat16)


def solution(mesh):
    return jax.shard_map(
        shards,
        mesh=mesh,
        in_specs=(
            P(("groups", "row"), "col", None, None, None),
            P(("groups", "row"), "col", None, None, None),
            P("row", "col", None, None, None),
        ),
        out_specs=P(("groups", "row"), "col", None, None, None),
        check_vma=False,
    )
```

profile of v0, /device:TPU:0, one launch (start us, length us, event | category | flops | bytes accessed | tf_op | source)
XLA Modules:
  0.0 410.3 jit_solution(6011335314331495683)
XLA Ops:
  2.1 1.2 broadcast_in_dim.7
  3.4 2.3 convert_element_type.82
  5.7 3.4 copy.13
  9.1 2.6 multiply_convert_fusion.1
  11.7 3.1 collective-permute-start
  14.8 2.1 collective-permute-start.1
  16.9 3.8 collective-permute-start.5
  27.4 1.0 fusion.598
  29.5 1.0 fusion.688
  30.5 1.0 fusion.689
  37.1 17.6 %collective-permute-done = bf16[1,2,9,184,184]{4,3,1,2,0:T(8,128)(2,1)S(1)} collective-permute-done((bf16[1,2,9,184,184]{4,3,1,2,0:T(8,128)(2,1)S(1)}, bf16[1,2,9,184,184]{4,3,1,2,0:T(8,128)(2,1)S(1)}, u32[]{:S(2)}, u32[]{:S(2)}) %collective-permute-start) | collective-permute-done | bytes 1218848 | tf_op jit(solution)/shard_map/ppermute | solution.py:15
  54.7 36.5 %collective-permute-done.1 = bf16[1,2,9,184,184]{4,3,1,2,0:T(8,128)(2,1)S(1)} collective-permute-done((bf16[1,2,9,184,184]{4,3,1,2,0:T(8,128)(2,1)S(1)}, bf16[1,2,9,184,184]{4,3,1,2,0:T(8,128)(2,1)S(1)}, u32[]{:S(2)}, u32[]{:S(2)}) %collective-permute-start.1) | collective-permute-done | bytes 1218848 | tf_op jit(solution)/shard_map/ppermute | solution.py:18
  91.2 1.2 pad_maximum_fusion
  92.4 2.5 fusion.695
  95.5 32.0 %collective-permute-done.4 = bf16[1,2,9,184,184]{4,3,1,2,0:T(8,128)(2,1)S(1)} collective-permute-done((bf16[1,2,9,184,184]{4,3,1,2,0:T(8,128)(2,1)S(1)}, bf16[1,2,9,184,184]{4,3,1,2,0:T(8,128)(2,1)S(1)}, u32[]{:S(2)}, u32[]{:S(2)}) %collective-permute-start.4) | collective-permute-done | bytes 1218848 | tf_op jit(solution)/shard_map/ppermute | solution.py:15
  127.4 34.9 %collective-permute-done.5 = bf16[1,2,9,184,184]{4,3,1,2,0:T(8,128)(2,1)S(1)} collective-permute-done((bf16[1,2,9,184,184]{4,3,1,2,0:T(8,128)(2,1)S(1)}, bf16[1,2,9,184,184]{4,3,1,2,0:T(8,128)(2,1)S(1)}, u32[]{:S(2)}, u32[]{:S(2)}) %collective-permute-start.5) | collective-permute-done | bytes 1218848 | tf_op jit(solution)/shard_map/ppermute | solution.py:18
  162.3 1.2 pad_maximum_fusion.1
  163.5 1.8 fusion.693
  169.5 52.0 %collective-permute-done.7 = bf16[3,1,9,184,184]{4,3,1,2,0:T(8,128)(2,1)S(1)} collective-permute-done((bf16[3,1,9,184,184]{4,3,1,2,0:T(8,128)(2,1)}, bf16[3,1,9,184,184]{4,3,1,2,0:T(8,128)(2,1)S(1)}, u32[]{:S(2)}, u32[]{:S(2)}) %collective-permute-start.7) | collective-permute-done | bytes 1828256 | tf_op jit(solution)/shard_map/ppermute | solution.py:18
  222.1 1.0 collective-permute-done.6
  249.1 1.3 fusion.174
  256.4 1.3 collective-permute-start.8
  257.8 2.5 collective-permute-start.9
  274.3 1.0 fusion.72
  280.3 1.0 fusion.86
  282.3 15.9 %collective-permute-done.8 = bf16[1,2,9,184,184]{4,3,1,2,0:T(8,128)(2,1)S(1)} collective-permute-done((bf16[1,2,9,184,184]{4,3,1,2,0:T(8,128)(2,1)S(1)}, bf16[1,2,9,184,184]{4,3,1,2,0:T(8,128)(2,1)S(1)}, u32[]{:S(2)}, u32[]{:S(2)}) %collective-permute-start.8) | collective-permute-done | bytes 1218848 | tf_op jit(solution)/shard_map/ppermute | solution.py:15
  298.2 34.7 %collective-permute-done.9 = bf16[1,2,9,184,184]{4,3,1,2,0:T(8,128)(2,1)S(1)} collective-permute-done((bf16[1,2,9,184,184]{4,3,1,2,0:T(8,128)(2,1)S(1)}, bf16[1,2,9,184,184]{4,3,1,2,0:T(8,128)(2,1)S(1)}, u32[]{:S(2)}, u32[]{:S(2)}) %collective-permute-start.9) | collective-permute-done | bytes 1218848 | tf_op jit(solution)/shard_map/ppermute | solution.py:18
  333.0 1.2 pad_maximum_fusion.2
  334.5 1.1 collective-permute-start.11
  337.5 53.4 %collective-permute-done.11 = bf16[3,1,9,184,184]{4,3,1,2,0:T(8,128)(2,1)S(1)} collective-permute-done((bf16[3,1,9,184,184]{4,3,1,2,0:T(8,128)(2,1)S(1)}, bf16[3,1,9,184,184]{4,3,1,2,0:T(8,128)(2,1)S(1)}, u32[]{:S(2)}, u32[]{:S(2)}) %collective-permute-start.11) | collective-permute-done | bytes 1828256 | tf_op jit(solution)/shard_map/ppermute | solution.py:18
  405.1 3.9 fusion.1
  409.0 1.3 copy.16
  (376 shorter events, 87.4 us)
Async XLA Ops:
  11.7 43.0 %collective-permute-start = (bf16[1,2,9,184,184]{4,3,1,2,0:T(8,128)(2,1)S(1)}, bf16[1,2,9,184,184]{4,3,1,2,0:T(8,128)(2,1)S(1)}, u32[]{:S(2)}, u32[]{:S(2)}) collective-permute-start(bf16[1,2,9,184,184]{4,3,1,2,0:T(8,128)(2,1)S(1)} %get-tuple-element.44), channel_id=1, source_target_pairs={{0,4},{4,8},{8,12},{12,0},{1,5},{5,9},{9,13},{13,1},{2,6},{6,10},{... | collective-permute-start | bytes 3656456 | tf_op jit(solution)/shard_map/ppermute | solution.py:15
  14.8 76.4 %collective-permute-start.1 = (bf16[1,2,9,184,184]{4,3,1,2,0:T(8,128)(2,1)S(1)}, bf16[1,2,9,184,184]{4,3,1,2,0:T(8,128)(2,1)S(1)}, u32[]{:S(2)}, u32[]{:S(2)}) collective-permute-start(bf16[1,2,9,184,184]{4,3,1,2,0:T(8,128)(2,1)S(1)} %get-tuple-element.44), channel_id=1, source_target_pairs={{4,0},{8,4},{12,8},{0,12},{5,1},{9,5},{13,9},{1,13},{6,2},{10,6},{... | collective-permute-start | bytes 3656456 | tf_op jit(solution)/shard_map/ppermute | solution.py:18
  16.9 110.6 %collective-permute-start.4 = (bf16[1,2,9,184,184]{4,3,1,2,0:T(8,128)(2,1)S(1)}, bf16[1,2,9,184,184]{4,3,1,2,0:T(8,128)(2,1)S(1)}, u32[]{:S(2)}, u32[]{:S(2)}) collective-permute-start(bf16[1,2,9,184,184]{4,3,1,2,0:T(8,128)(2,1)S(1)} %get-tuple-element.43), channel_id=1, source_target_pairs={{0,4},{4,8},{8,12},{12,0},{1,5},{5,9},{9,13},{13,1},{2,6},{6,10},{... | collective-permute-start | bytes 3656456 | tf_op jit(solution)/shard_map/ppermute | solution.py:15
  16.9 145.4 %collective-permute-start.5 = (bf16[1,2,9,184,184]{4,3,1,2,0:T(8,128)(2,1)S(1)}, bf16[1,2,9,184,184]{4,3,1,2,0:T(8,128)(2,1)S(1)}, u32[]{:S(2)}, u32[]{:S(2)}) collective-permute-start(bf16[1,2,9,184,184]{4,3,1,2,0:T(8,128)(2,1)S(1)} %get-tuple-element.43), channel_id=1, source_target_pairs={{4,0},{8,4},{12,8},{0,12},{5,1},{9,5},{13,9},{1,13},{6,2},{10,6},{... | collective-permute-start | bytes 3656456 | tf_op jit(solution)/shard_map/ppermute | solution.py:18
  95.0 136.9 %collective-permute-start.3 = (bf16[3,1,9,184,184]{4,3,1,2,0:T(8,128)(2,1)}, bf16[3,1,9,184,184]{4,3,1,2,0:T(8,128)(2,1)S(1)}, u32[]{:S(2)}, u32[]{:S(2)}) collective-permute-start(bf16[3,1,9,184,184]{4,3,1,2,0:T(8,128)(2,1)} %get-tuple-element.41), channel_id=1, source_target_pairs={{1,0},{2,1},{3,2},{0,3},{5,4},{6,5},{7,6},{4,7},{9,8},{10,9},{11,1... | collective-permute-start | bytes 5484680 | tf_op jit(solution)/shard_map/ppermute | solution.py:18
  95.0 140.9 %collective-permute-start.2 = (bf16[3,1,9,184,184]{4,3,1,2,0:T(8,128)(2,1)}, bf16[3,1,9,184,184]{4,3,1,2,0:T(8,128)(2,1)S(1)}, u32[]{:S(2)}, u32[]{:S(2)}) collective-permute-start(bf16[3,1,9,184,184]{4,3,1,2,0:T(8,128)(2,1)} %get-tuple-element.42), channel_id=1, source_target_pairs={{0,1},{1,2},{2,3},{3,0},{4,5},{5,6},{6,7},{7,4},{8,9},{9,10},{10,1... | collective-permute-start | bytes 5484680 | tf_op jit(solution)/shard_map/ppermute | solution.py:15
  165.3 56.2 %collective-permute-start.7 = (bf16[3,1,9,184,184]{4,3,1,2,0:T(8,128)(2,1)}, bf16[3,1,9,184,184]{4,3,1,2,0:T(8,128)(2,1)S(1)}, u32[]{:S(2)}, u32[]{:S(2)}) collective-permute-start(bf16[3,1,9,184,184]{4,3,1,2,0:T(8,128)(2,1)} %get-tuple-element.37), channel_id=1, source_target_pairs={{1,0},{2,1},{3,2},{0,3},{5,4},{6,5},{7,6},{4,7},{9,8},{10,9},{11,1... | collective-permute-start | bytes 5484680 | tf_op jit(solution)/shard_map/ppermute | solution.py:18
  165.8 57.3 %collective-permute-start.6 = (bf16[3,1,9,184,184]{4,3,1,2,0:T(8,128)(2,1)S(1)}, bf16[3,1,9,184,184]{4,3,1,2,0:T(8,128)(2,1)S(1)}, u32[]{:S(2)}, u32[]{:S(2)}) collective-permute-start(bf16[3,1,9,184,184]{4,3,1,2,0:T(8,128)(2,1)S(1)} %get-tuple-element.38), channel_id=1, source_target_pairs={{0,1},{1,2},{2,3},{3,0},{4,5},{5,6},{6,7},{7,4},{8,9},{9,10},{10,1... | collective-permute-start | bytes 5484680 | tf_op jit(solution)/shard_map/ppermute | solution.py:15
  221.7 2.4 copy-start.18
  221.7 6.7 %copy-start.50 = (bf16[2,184,184]{2,1,0:T(8,128)(2,1)}, bf16[2,184,184]{2,1,0:T(8,128)(2,1)S(1)}, u32[]{:S(2)}) copy-start(bf16[2,184,184]{2,1,0:T(8,128)(2,1)S(1)} %get-tuple-element.5) | copy-start | bytes 406276
  223.3 3.0 copy-start.26
  223.3 11.5 %copy-start.2 = (bf16[2,184,184]{2,1,0:T(8,128)(2,1)}, bf16[2,184,184]{2,1,0:T(8,128)(2,1)S(1)}, u32[]{:S(2)}) copy-start(bf16[2,184,184]{2,1,0:T(8,128)(2,1)S(1)} %get-tuple-element.15) | copy-start | bytes 406276
  223.3 12.3 %copy-start = (bf16[2,184,184]{2,1,0:T(8,128)(2,1)}, bf16[2,184,184]{2,1,0:T(8,128)(2,1)S(1)}, u32[]{:S(2)}) copy-start(bf16[2,184,184]{2,1,0:T(8,128)(2,1)S(1)} %get-tuple-element.13) | copy-start | bytes 406276
  223.9 2.5 copy-start.28
  223.9 5.5 %copy-start.20 = (bf16[2,184,184]{2,1,0:T(8,128)(2,1)}, bf16[2,184,184]{2,1,0:T(8,128)(2,1)S(1)}, u32[]{:S(2)}) copy-start(bf16[2,184,184]{2,1,0:T(8,128)(2,1)S(1)} %get-tuple-element.9) | copy-start | bytes 406276
  223.9 10.7 %copy-start.4 = (bf16[2,184,184]{2,1,0:T(8,128)(2,1)}, bf16[2,184,184]{2,1,0:T(8,128)(2,1)S(1)}, u32[]{:S(2)}) copy-start(bf16[2,184,184]{2,1,0:T(8,128)(2,1)S(1)} %get-tuple-element.10) | copy-start | bytes 406276
  225.0 2.3 copy-start.32
  225.0 6.2 %copy-start.52 = (bf16[2,184,184]{2,1,0:T(8,128)(2,1)}, bf16[2,184,184]{2,1,0:T(8,128)(2,1)S(1)}, u32[]{:S(2)}) copy-start(bf16[2,184,184]{2,1,0:T(8,128)(2,1)S(1)} %get-tuple-element.23) | copy-start | bytes 406276
  225.0 9.3 %copy-start.6 = (bf16[2,184,184]{2,1,0:T(8,128)(2,1)}, bf16[2,184,184]{2,1,0:T(8,128)(2,1)S(1)}, u32[]{:S(2)}) copy-start(bf16[2,184,184]{2,1,0:T(8,128)(2,1)S(1)} %get-tuple-element.21) | copy-start | bytes 406276
  226.0 3.2 copy-start.30
  226.0 5.6 %copy-start.48 = (bf16[2,184,184]{2,1,0:T(8,128)(2,1)}, bf16[2,184,184]{2,1,0:T(8,128)(2,1)S(1)}, u32[]{:S(2)}) copy-start(bf16[2,184,184]{2,1,0:T(8,128)(2,1)S(1)} %get-tuple-element.20) | copy-start | bytes 406276
  226.0 7.3 %copy-start.8 = (bf16[2,184,184]{2,1,0:T(8,128)(2,1)}, bf16[2,184,184]{2,1,0:T(8,128)(2,1)S(1)}, u32[]{:S(2)}) copy-start(bf16[2,184,184]{2,1,0:T(8,128)(2,1)S(1)} %get-tuple-element.19) | copy-start | bytes 406276
  227.1 2.6 copy-start.16
  227.1 4.4 %copy-start.10 = (bf16[2,184,184]{2,1,0:T(8,128)(2,1)}, bf16[2,184,184]{2,1,0:T(8,128)(2,1)S(1)}, u32[]{:S(2)}) copy-start(bf16[2,184,184]{2,1,0:T(8,128)(2,1)S(1)} %get-tuple-element.25) | copy-start | bytes 406276
  227.7 2.5 copy-start.54
  256.4 41.8 %collective-permute-start.8 = (bf16[1,2,9,184,184]{4,3,1,2,0:T(8,128)(2,1)S(1)}, bf16[1,2,9,184,184]{4,3,1,2,0:T(8,128)(2,1)S(1)}, u32[]{:S(2)}, u32[]{:S(2)}) collective-permute-start(bf16[1,2,9,184,184]{4,3,1,2,0:T(8,128)(2,1)S(1)} %get-tuple-element.34), channel_id=1, source_target_pairs={{0,4},{4,8},{8,12},{12,0},{1,5},{5,9},{9,13},{13,1},{2,6},{6,10},{... | collective-permute-start | bytes 3656456 | tf_op jit(solution)/shard_map/ppermute | solution.py:15
  257.8 75.2 %collective-permute-start.9 = (bf16[1,2,9,184,184]{4,3,1,2,0:T(8,128)(2,1)S(1)}, bf16[1,2,9,184,184]{4,3,1,2,0:T(8,128)(2,1)S(1)}, u32[]{:S(2)}, u32[]{:S(2)}) collective-permute-start(bf16[1,2,9,184,184]{4,3,1,2,0:T(8,128)(2,1)S(1)} %get-tuple-element.34), channel_id=1, source_target_pairs={{4,0},{8,4},{12,8},{0,12},{5,1},{9,5},{13,9},{1,13},{6,2},{10,6},{... | collective-permute-start | bytes 3656456 | tf_op jit(solution)/shard_map/ppermute | solution.py:18
  265.1 3.8 copy-start.51
  267.0 2.3 copy-start.25
  278.4 1.9 copy-start.1
  334.5 56.4 %collective-permute-start.11 = (bf16[3,1,9,184,184]{4,3,1,2,0:T(8,128)(2,1)S(1)}, bf16[3,1,9,184,184]{4,3,1,2,0:T(8,128)(2,1)S(1)}, u32[]{:S(2)}, u32[]{:S(2)}) collective-permute-start(bf16[3,1,9,184,184]{4,3,1,2,0:T(8,128)(2,1)S(1)} %get-tuple-element.39), channel_id=1, source_target_pairs={{1,0},{2,1},{3,2},{0,3},{5,4},{6,5},{7,6},{4,7},{9,8},{10,9},{11,1... | collective-permute-start | bytes 5484680 | tf_op jit(solution)/shard_map/ppermute | solution.py:18
  335.6 56.6 %collective-permute-start.10 = (bf16[3,1,9,184,184]{4,3,1,2,0:T(8,128)(2,1)S(1)}, bf16[3,1,9,184,184]{4,3,1,2,0:T(8,128)(2,1)S(1)}, u32[]{:S(2)}, u32[]{:S(2)}) collective-permute-start(bf16[3,1,9,184,184]{4,3,1,2,0:T(8,128)(2,1)S(1)} %get-tuple-element.40), channel_id=1, source_target_pairs={{0,1},{1,2},{2,3},{3,0},{4,5},{5,6},{6,7},{7,4},{8,9},{9,10},{10,1... | collective-permute-start | bytes 5484680 | tf_op jit(solution)/shard_map/ppermute | solution.py:15
  (62 other events, 63.7 us)
where the time goes:
time: 412 us; the launch traced here: 410 us
  waiting for transfers between devices  279 us (68%)
  matrix products  67.7 us (16%)
  local copies, waits for them, and re-layouts  33.5 us (8%)
  starting transfers between devices  15 us (4%)
  other arithmetic  13.4 us (3%)
    ppermute x6, waiting for transfers between devices, with_halo(): lax.ppermute(lax.slice_in_dim(block, 0, width, axis=dim), axis, backward)  212 us
    dot_general x196, matrix products, tile_product(): jnp.einsum('xyab,xybc->xyac', left_tile, moved[:, :, second_off], preferr...  67.7 us
    ppermute x6, waiting for transfers between devices, with_halo(): lax.ppermute(lax.slice_in_dim(block, block.shape[dim] - width, None, axis...  67.1 us
    unnamed x164, local copies, waits for them, and re-layouts  19.3 us
    ppermute x6, starting transfers between devices, with_halo(): lax.ppermute(lax.slice_in_dim(block, 0, width, axis=dim), axis, backward)  10.1 us
  transfers between devices with their start and end apart: 12, of which 10 were waited for; matrix products, arithmetic and copies ran while one was open for 14% of the time, Pallas kernels for 0%

commit v1 on v0

v1 whole, which is shorter than its diff:
```python
import functools

import jax
import jax.numpy as jnp
from jax import lax
from jax.experimental import pallas as pl
from jax.experimental.pallas import tpu as pltpu
from jax.sharding import PartitionSpec as P

BLOCK = 23
MESH = pl.DeviceIdType.MESH
ORDER = (0, 1, 2, 6, 7, 8, 3, 5, 4)


def shifts(offset):
    return (offset // 3 - 1, offset % 3 - 1)


def sources(target):
    out = []
    for first in range(9):
        fx, fy = shifts(first)
        tx, ty = shifts(target)
        sx, sy = tx - fx, ty - fy
        if abs(sx) <= 1 and abs(sy) <= 1:
            out.append((first, (sx + 1) * 3 + sy + 1))
    return out


def halo_plan():
    plan = []
    for dr in (1, -1):
        plan.append((dr, 0, 0, 3, 3))
        plan.append((dr, 0, 1, 4, 2))
    for dr in (1, -1):
        plan.append((dr, 1, 1, 4, 1))
        plan.append((dr, -1, 0, 4, 1))
    for first, count in ((1, 2), (4, 1), (7, 2)):
        plan.append((0, 1, 1, first, count))
    for first, count in ((0, 2), (4, 1), (6, 2)):
        plan.append((0, -1, 0, first, count))
    return plan


def place(col, offset):
    sx, sy = shifts(offset)
    y = col + sy
    return sx, y // 2, y % 2


def is_local(col, offset):
    sx, dc, _ = place(col, offset)
    return sx == 0 and dc == 0


HALO = halo_plan()
REMOTE = [(c, o) for o in ORDER for c in range(2) if not is_local(c, o)]


def kernel(
    rows, cols, base, tangent, pattern, out,
    q, p, mask, r32, rb, rt, f, gt, g, s,
    h_send, h_recv, r_send, r_recv, g_send, g_recv,
):
    group = lax.axis_index("groups")
    row = lax.axis_index("row")
    col = lax.axis_index("col")
    tile = base.shape[-1]

    def device(dr, dc):
        return (group, lax.rem(row + dr + rows, rows), lax.rem(col + dc + cols, cols))

    barrier = pltpu.get_barrier_semaphore()
    around = [(a, b) for a in (-1, 0, 1) for b in (-1, 0, 1) if (a, b) != (0, 0)]
    for dr, dc in around:
        pl.semaphore_signal(barrier, inc=1, device_id=device(dr, dc), device_id_type=MESH)

    blocks = pattern.shape[-1]
    up_r = lax.broadcasted_iota(jnp.int32, (tile, blocks), 0)
    up_c = lax.broadcasted_iota(jnp.int32, (tile, blocks), 1) * BLOCK
    up = ((up_r >= up_c) & (up_r < up_c + BLOCK)).astype(jnp.float32).astype(jnp.bfloat16)
    wide_r = lax.broadcasted_iota(jnp.int32, (blocks, tile), 0) * BLOCK
    wide_c = lax.broadcasted_iota(jnp.int32, (blocks, tile), 1)
    wide = ((wide_c >= wide_r) & (wide_c < wide_r + BLOCK)).astype(jnp.float32).astype(jnp.bfloat16)

    @pl.loop(0, 18)
    def _(i):
        c = i // 9
        o = i % 9
        pat = pattern[0, c, o].astype(jnp.float32).astype(jnp.bfloat16)
        part = jnp.dot(pat, wide, preferred_element_type=jnp.float32).astype(jnp.bfloat16)
        m = jnp.dot(up, part, preferred_element_type=jnp.float32)
        mask[c, o] = m.astype(jnp.bfloat16)
        q[1, 1 + c, o] = (base[0, c, o].astype(jnp.float32) * m).astype(jnp.bfloat16)

    pl.semaphore_wait(barrier, 8)

    halo = []
    for k, (dr, dc, c, first, count) in enumerate(HALO):
        copy = pltpu.make_async_remote_copy(
            src_ref=q.at[1, 1 + c, pl.ds(first, count)],
            dst_ref=q.at[1 - dr, 1 + c - 2 * dc, pl.ds(first, count)],
            send_sem=h_send.at[k],
            recv_sem=h_recv.at[k],
            device_id=device(dr, dc),
            device_id_type=MESH,
        )
        copy.start()
        halo.append(copy)

    @pl.loop(0, 18)
    def _(i):
        c = i // 9
        o = i % 9
        m = mask[c, o].astype(jnp.float32)
        p[c, o] = (tangent[0, c, o].astype(jnp.float32) * m).astype(jnp.bfloat16)

    def flip(node, o):
        sx, sy = shifts(o)
        nx, ny = node
        q[1 + nx + sx, 1 + ny + sy, 8 - o] = q[1 + nx, 1 + ny, o].T

    for c in range(2):
        for o in range(9):
            if not is_local(c, o):
                flip((0, c), o)

    for copy, (dr, dc, c, first, count) in zip(halo, HALO):
        copy.wait_recv()
        for o in range(first, first + count):
            if o != 4:
                flip((-dr, c - 2 * dc), o)

    def product(left, c, target):
        total = None
        for first, second in sources(target):
            ax, ay = shifts(first)
            term = jnp.dot(
                left[c, first], q[1 + ax, c + 1 + ay, second],
                preferred_element_type=jnp.float32,
            )
            total = term if total is None else total + term
        return total

    def returned(src, dst, send, recv, c, o):
        dr, dc, other = place(c, o)
        k = REMOTE.index((c, o))
        return pltpu.make_async_remote_copy(
            src_ref=src.at[c, o],
            dst_ref=dst.at[other, 8 - o],
            send_sem=send.at[k],
            recv_sem=recv.at[k],
            device_id=device(dr, dc),
            device_id_type=MESH,
        )

    def hand_over(src, dst, send, recv, o):
        for c in range(2):
            if is_local(c, o):
                dst[place(c, o)[2], 8 - o] = src[c, o]
            else:
                returned(src, dst, send, recv, c, o).start()

    for o in ORDER:
        @pl.loop(0, 2)
        def _(c):
            total = product(p, c, o) * mask[c, o].astype(jnp.float32)
            r32[c, o] = total
            half = total.astype(jnp.bfloat16)
            rb[c, o] = half
            rt[c, o] = half.T

        hand_over(rt, f, r_send, r_recv, o)

    for o in ORDER:
        @pl.loop(0, 2)
        def _(c):
            g[c, o] = product(rb, c, o).astype(jnp.bfloat16).T

        hand_over(g, gt, g_send, g_recv, o)

    for c, o in REMOTE:
        returned(rt, f, r_send, r_recv, c, o).wait_recv()

    @pl.loop(0, 18)
    def _(i):
        c = i // 9
        o = i % 9
        total = r32[c, o] + f[c, o].astype(jnp.float32)
        r32[c, o] = 3.0 * total
        s[c, o] = total.astype(jnp.bfloat16)

    for o in ORDER:
        @pl.loop(0, 2)
        def _(c):
            r32[c, o] = r32[c, o] - 2.0 * mask[c, o].astype(jnp.float32) * product(s, c, o)

    for c, o in REMOTE:
        returned(g, gt, g_send, g_recv, c, o).wait_recv()

    @pl.loop(0, 18)
    def _(i):
        c = i // 9
        o = i % 9
        m = mask[c, o].astype(jnp.float32)
        total = r32[c, o] - 2.0 * m * gt[c, o].astype(jnp.float32)
        out[0, c, o] = total.astype(jnp.bfloat16)

    for copy in halo:
        copy.wait_send()
    for c, o in REMOTE:
        returned(rt, f, r_send, r_recv, c, o).wait_send()
        returned(g, gt, g_send, g_recv, c, o).wait_send()


def shards(rows, cols, base_density, tangent_density, pattern):
    tile = base_density.shape[-1]
    tiles = (2, 9, tile, tile)
    vmem = pl.BlockSpec(memory_space=pltpu.VMEM)
    small = pltpu.VMEM(tiles, jnp.bfloat16)
    remote = len(REMOTE)
    return pl.pallas_call(
        functools.partial(kernel, rows, cols),
        out_shape=jax.ShapeDtypeStruct(base_density.shape, jnp.bfloat16),
        in_specs=[vmem] * 3,
        out_specs=vmem,
        scratch_shapes=[
            pltpu.VMEM((3, 4, 9, tile, tile), jnp.bfloat16),
            small,
            small,
            pltpu.VMEM(tiles, jnp.float32),
            small,
            small,
            small,
            small,
            small,
            small,
            pltpu.SemaphoreType.DMA((len(HALO),)),
            pltpu.SemaphoreType.DMA((len(HALO),)),
            pltpu.SemaphoreType.DMA((remote,)),
            pltpu.SemaphoreType.DMA((remote,)),
            pltpu.SemaphoreType.DMA((remote,)),
            pltpu.SemaphoreType.DMA((remote,)),
        ],
        compiler_params=pltpu.CompilerParams(
            collective_id=0, has_side_effects=True, vmem_limit_bytes=56 * 2**20
        ),
        name="tangent_step",
    )(base_density, tangent_density, pattern)


def solution(mesh):
    spec = P(("groups", "row"), "col", None, None, None)
    return jax.shard_map(
        functools.partial(shards, mesh.shape["row"], mesh.shape["col"]),
        mesh=mesh,
        in_specs=(spec, spec, P("row", "col", None, None, None)),
        out_specs=spec,
        check_vma=False,
    )
```

time: 412 us -> 100 us (0.24)
  waiting for transfers between devices: 279 us -> 0 us
  Pallas kernels: 0 us -> 95.6 us
  matrix products: 67.7 us -> 0 us
  local copies, waits for them, and re-layouts: 33.5 us -> 4.38 us
  starting transfers between devices: 15 us -> 0 us
  other arithmetic: 13.4 us -> 0 us
    ppermute x12 -> x0, waiting for transfers between devices: 279 us -> none  [the longest x6 212 us: with_halo(): lax.ppermute(lax.slice_in_dim(block, 0, width, axis=dim), axis, backward)]
    pallas_call x0 -> x1, Pallas kernels: none -> 95.6 us  [shards(): pl.pallas_call(functools.partial(kernel, rows, cols), out_shape=jax.Shape...]
    dot_general x196 -> x0, matrix products: 67.7 us -> none  [tile_product(): jnp.einsum('xyab,xybc->xyac', left_tile, moved[:, :, second_off], preferr...]
    ppermute x12 -> x0, starting transfers between devices: 15 us -> none  [the longest x6 10.1 us: with_halo(): lax.ppermute(lax.slice_in_dim(block, 0, width, axis=dim), axis, backward)]
    unnamed x164 -> x2, local copies, waits for them, and re-layouts: 19.3 us -> 4.38 us
    convert_element_type x4 -> x0, other arithmetic: 8.66 us -> none  [the longest x1 3.93 us: shards(): return result.astype(jnp.bfloat16)]
    convert_element_type x5 -> x0, local copies, waits for them, and re-layouts: 8.08 us -> none  [the longest x4 6.79 us: expand(): return wide.astype(jnp.float32)]
    slice x3 -> x0, local copies, waits for them, and re-layouts: 4.69 us -> none  [with_halo(): lax.slice_in_dim(block, 0, width, axis=dim)]
  transfers between devices with their start and end apart: 12 -> 0, of which waited for: 10 -> 0; matrix products, arithmetic and copies ran while one was open for 14% -> 0% of each run, Pallas kernels for 0% -> 0%
where the time goes in v1:
time: 100 us
  Pallas kernels  95.6 us (96%)
  local copies, waits for them, and re-layouts  4.38 us (4%)
    pallas_call x1, Pallas kernels, shards(): pl.pallas_call(functools.partial(kernel, rows, cols), out_shape=jax.Shape...  95.6 us
    unnamed x2, local copies, waits for them, and re-layouts  4.38 us

profile of v1, /device:TPU:0, one launch (start us, length us, event | category | flops | bytes accessed | tf_op | source)
XLA Modules:
  0.0 100.0 jit_solution(11526270839436467793)
XLA Ops:
  0.0 1.6 %copy.4.pattern = s32[1,2,9,8,8]{4,3,2,1,0:T(8,128)} copy(s32[1,2,9,8,8]{2,4,3,1,0:T(8,128)} %param.5) | data formatting | bytes 9216 | tf_op args[2]
  1.6 95.6 %tangent_step.1 = bf16[1,2,9,184,184]{4,3,2,1,0:T(8,128)(2,1)} custom-call(bf16[1,2,9,184,184]{4,3,2,1,0:T(8,128)(2,1)} %base.1, bf16[1,2,9,184,184]{4,3,2,1,0:T(8,128)(2,1)} %tangent.1, s32[1,2,9,8,8]{4,3,2,1,0:T(8,128)} %copy.4.pattern), custom_call_target="tpu_custom_call" | custom-call | tf_op jit(solution)/shard_map/tangent_step/pallas_call | solution.py:222
  97.3 2.7 %copy.6 = bf16[1,2,9,184,184]{4,3,2,1,0:T(8,128)(2,1)} copy(bf16[1,2,9,184,184]{4,3,2,1,0:T(8,128)(2,1)} %tangent_step.1) | data formatting | bytes 2437632

commit v2 on v1

v2 whole, which is shorter than its diff:
```python
import functools

import jax
import jax.numpy as jnp
from jax import lax
from jax.experimental import pallas as pl
from jax.experimental.pallas import tpu as pltpu
from jax.sharding import PartitionSpec as P

BLOCK = 23
MESH = pl.DeviceIdType.MESH
ORDER = (0, 1, 2, 6, 7, 8, 3, 5, 4)


def shifts(offset):
    return (offset // 3 - 1, offset % 3 - 1)


def sources(target):
    out = []
    for first in range(9):
        fx, fy = shifts(first)
        tx, ty = shifts(target)
        sx, sy = tx - fx, ty - fy
        if abs(sx) <= 1 and abs(sy) <= 1:
            out.append((first, (sx + 1) * 3 + sy + 1))
    return out


def side_plan():
    plan = [(1, 1, first, count) for first, count in ((1, 2), (4, 1), (7, 2))]
    plan += [(-1, 0, first, count) for first, count in ((0, 2), (4, 1), (6, 2))]
    return plan


PASS_ON = ((1, 1, 4, 2), (-1, 0, 4, 1))
LANES = 128
FOLD = 96


def place(col, offset):
    sx, sy = shifts(offset)
    y = col + sy
    return sx, y // 2, y % 2


def is_local(col, offset):
    sx, dc, _ = place(col, offset)
    return sx == 0 and dc == 0


SIDE = side_plan()
STEPS = (1, -1)
REMOTE = [(c, o) for o in ORDER for c in range(2) if not is_local(c, o)]


def fold(ref, value):
    tile = value.shape[-1]
    rest = tile - LANES
    ref[:, 0:rest] = value[0:FOLD, LANES:tile]
    ref[0 : tile - FOLD, LANES // 2 : LANES // 2 + rest] = value[FOLD:tile, LANES:tile]


def unfold(ref, folded):
    tile = ref.shape[-1]
    rest = tile - LANES
    ref[0:FOLD, LANES:tile] = folded[:, 0:rest]
    ref[FOLD:tile, LANES:tile] = folded[0 : tile - FOLD, LANES // 2 : LANES // 2 + rest]


def kernel(
    rows, cols, base, tangent, pattern, out,
    q, p, mask, r32, rb, rt, f, gt, g, s,
    own_fold, halo_fold, rt_fold, f_fold, g_fold, gt_fold,
    z_send, z_recv, h_send, h_recv, n_send, n_recv, r_send, r_recv, g_send, g_recv,
):
    group = lax.axis_index("groups")
    row = lax.axis_index("row")
    col = lax.axis_index("col")
    tile = base.shape[-1]

    def device(dr, dc):
        return (group, lax.rem(row + dr + rows, rows), lax.rem(col + dc + cols, cols))

    barrier = pltpu.get_barrier_semaphore()
    around = [(a, b) for a in (-1, 0, 1) for b in (-1, 0, 1) if (a, b) != (0, 0)]
    for dr, dc in around:
        pl.semaphore_signal(barrier, inc=1, device_id=device(dr, dc), device_id_type=MESH)

    blocks = pattern.shape[-1]
    up_r = lax.broadcasted_iota(jnp.int32, (tile, blocks), 0)
    up_c = lax.broadcasted_iota(jnp.int32, (tile, blocks), 1) * BLOCK
    up = ((up_r >= up_c) & (up_r < up_c + BLOCK)).astype(jnp.float32).astype(jnp.bfloat16)
    wide_r = lax.broadcasted_iota(jnp.int32, (blocks, tile), 0) * BLOCK
    wide_c = lax.broadcasted_iota(jnp.int32, (blocks, tile), 1)
    wide = ((wide_c >= wide_r) & (wide_c < wide_r + BLOCK)).astype(jnp.float32).astype(jnp.bfloat16)

    def prepare(c, o):
        pat = pattern[0, c, o].astype(jnp.float32).astype(jnp.bfloat16)
        part = jnp.dot(pat, wide, preferred_element_type=jnp.float32).astype(jnp.bfloat16)
        m = jnp.dot(up, part, preferred_element_type=jnp.float32)
        mask[c, o] = m.astype(jnp.bfloat16)
        kept = (base[0, c, o].astype(jnp.float32) * m).astype(jnp.bfloat16)
        q[1, 1 + c, o] = kept
        return kept

    @pl.loop(0, 2)
    def _(c):
        for e in range(2):
            fold(own_fold.at[c, e], prepare(c, 4 + e))

    pl.semaphore_wait(barrier, 8)

    def over_rows(k):
        left = (pl.ds(1, 2), pl.ds(4, 2), slice(None), pl.ds(0, LANES))
        return [
            pltpu.make_async_remote_copy(
                src_ref=q.at[(1,) + left],
                dst_ref=q.at[(1 - STEPS[k],) + left],
                send_sem=z_send.at[k, 0],
                recv_sem=z_recv.at[k, 0],
                device_id=device(STEPS[k], 0),
                device_id_type=MESH,
            ),
            pltpu.make_async_remote_copy(
                src_ref=own_fold,
                dst_ref=halo_fold.at[k],
                send_sem=z_send.at[k, 1],
                recv_sem=z_recv.at[k, 1],
                device_id=device(STEPS[k], 0),
                device_id_type=MESH,
            ),
        ]

    def within_row(x, dc, c, first, count, send, recv):
        return pltpu.make_async_remote_copy(
            src_ref=q.at[x, 1 + c, pl.ds(first, count)],
            dst_ref=q.at[x, 1 + c - 2 * dc, pl.ds(first, count)],
            send_sem=send,
            recv_sem=recv,
            device_id=device(0, dc),
            device_id_type=MESH,
        )

    halo = [over_rows(k) for k in range(2)]
    for pair in halo:
        for copy in pair:
            copy.start()

    @pl.loop(0, 2)
    def _(c):
        for o in (0, 1, 2, 3, 6, 7, 8):
            prepare(c, o)

    side = []
    for k, (dc, c, first, count) in enumerate(SIDE):
        copy = within_row(1, dc, c, first, count, h_send.at[k], h_recv.at[k])
        copy.start()
        side.append(copy)

    @pl.loop(0, 18)
    def _(i):
        c = i // 9
        o = i % 9
        m = mask[c, o].astype(jnp.float32)
        p[c, o] = (tangent[0, c, o].astype(jnp.float32) * m).astype(jnp.bfloat16)

    def flip(node, o):
        sx, sy = shifts(o)
        nx, ny = node
        q[1 + nx + sx, 1 + ny + sy, 8 - o] = q[1 + nx, 1 + ny, o].T

    for c in range(2):
        for o in range(9):
            if not is_local(c, o):
                flip((0, c), o)

    for copy, (dc, c, first, count) in zip(side, SIDE):
        copy.wait_recv()
        for o in range(first, first + count):
            if o != 4:
                flip((0, c - 2 * dc), o)

    def product(left, c, target, near=None):
        total = None
        for first, second in sources(target):
            ax, ay = shifts(first)
            if near is not None and near != (ax == 0 or shifts(target)[0] == 0):
                continue
            term = jnp.dot(
                left[c, first], q[1 + ax, c + 1 + ay, second],
                preferred_element_type=jnp.float32,
            )
            total = term if total is None else total + term
        return total

    def returned(src, dst, src_fold, dst_fold, send, recv, c, o):
        dr, dc, other = place(c, o)
        k = REMOTE.index((c, o))
        left = (slice(None), pl.ds(0, LANES))
        pairs = (
            (src.at[(c, o) + left], dst.at[(other, 8 - o) + left]),
            (src_fold.at[c, o], dst_fold.at[other, 8 - o]),
        )
        return [
            pltpu.make_async_remote_copy(
                src_ref=here,
                dst_ref=there,
                send_sem=send.at[k, i],
                recv_sem=recv.at[k, i],
                device_id=device(dr, dc),
                device_id_type=MESH,
            )
            for i, (here, there) in enumerate(pairs)
        ]

    back_r = functools.partial(returned, rt, f, rt_fold, f_fold, r_send, r_recv)
    back_g = functools.partial(returned, g, gt, g_fold, gt_fold, g_send, g_recv)

    def hand_over(back, src, dst, c, o):
        if is_local(c, o):
            dst[place(c, o)[2], 8 - o] = src[c, o]
        else:
            for copy in back(c, o):
                copy.start()

    def finish_r(c, o, total):
        total = total * mask[c, o].astype(jnp.float32)
        r32[c, o] = total
        half = total.astype(jnp.bfloat16)
        rb[c, o] = half
        turned = half.T
        rt[c, o] = turned
        fold(rt_fold.at[c, o], turned)

    for o in (3, 5, 4):
        @pl.loop(0, 2)
        def _(c):
            finish_r(c, o, product(p, c, o, True))

        for c in range(2):
            hand_over(back_r, rt, f, c, o)

    for o in (0, 1, 2, 6, 7, 8):
        @pl.loop(0, 2)
        def _(c):
            r32[c, o] = product(p, c, o, True)

    passed = []
    for k, dr in enumerate(STEPS):
        x = 1 - dr
        for copy in halo[k]:
            copy.wait_recv()
        for c in range(2):
            for e in range(2):
                unfold(q.at[x, 1 + c, 4 + e], halo_fold.at[k, c, e])
        for i, (dc, c, first, count) in enumerate(PASS_ON):
            copy = within_row(x, dc, c, first, count, n_send.at[k, i], n_recv.at[k, i])
            copy.start()
            passed.append(copy)
        flip((-dr, 0), 5)
        flip((-dr, 1), 5)
        for c, sy in ((1, 0), (1, -1), (0, 1)):
            o = (x * 3) + sy + 1
            finish_r(c, o, r32[c, o] + product(p, c, o, False))
            hand_over(back_r, rt, f, c, o)

    for copy in passed:
        copy.wait_recv()
    for dr in STEPS:
        x = 1 - dr
        flip((-dr, -1), 5)
        for c, sy in ((0, 0), (0, -1), (1, 1)):
            o = (x * 3) + sy + 1
            finish_r(c, o, r32[c, o] + product(p, c, o, False))
            hand_over(back_r, rt, f, c, o)

    for o in ORDER:
        @pl.loop(0, 2)
        def _(c):
            turned = product(rb, c, o).astype(jnp.bfloat16).T
            g[c, o] = turned
            fold(g_fold.at[c, o], turned)

        for c in range(2):
            hand_over(back_g, g, gt, c, o)

    for c, o in REMOTE:
        for copy in back_r(c, o):
            copy.wait_recv()
        other = place(c, o)[2]
        unfold(f.at[other, 8 - o], f_fold.at[other, 8 - o])

    @pl.loop(0, 18)
    def _(i):
        c = i // 9
        o = i % 9
        total = r32[c, o] + f[c, o].astype(jnp.float32)
        r32[c, o] = 3.0 * total
        s[c, o] = total.astype(jnp.bfloat16)

    for o in ORDER:
        @pl.loop(0, 2)
        def _(c):
            r32[c, o] = r32[c, o] - 2.0 * mask[c, o].astype(jnp.float32) * product(s, c, o)

    def finish(c, o):
        m = mask[c, o].astype(jnp.float32)
        total = r32[c, o] - 2.0 * m * gt[c, o].astype(jnp.float32)
        out[0, c, o] = total.astype(jnp.bfloat16)

    for o in ORDER:
        for c in range(2):
            if is_local(c, o):
                finish(place(c, o)[2], 8 - o)

    for c, o in REMOTE:
        other = place(c, o)[2]
        for copy in back_g(c, o):
            copy.wait_recv()
        unfold(gt.at[other, 8 - o], gt_fold.at[other, 8 - o])
        finish(other, 8 - o)

    for copy in halo[0] + halo[1] + side + passed:
        copy.wait_send()
    for c, o in REMOTE:
        for copy in back_r(c, o) + back_g(c, o):
            copy.wait_send()


def shards(rows, cols, base_density, tangent_density, pattern):
    tile = base_density.shape[-1]
    tiles = (2, 9, tile, tile)
    vmem = pl.BlockSpec(memory_space=pltpu.VMEM)
    small = pltpu.VMEM(tiles, jnp.bfloat16)
    folded = pltpu.VMEM((2, 9, FOLD, LANES), jnp.bfloat16)
    dma = pltpu.SemaphoreType.DMA
    remote = len(REMOTE)
    return pl.pallas_call(
        functools.partial(kernel, rows, cols),
        out_shape=jax.ShapeDtypeStruct(base_density.shape, jnp.bfloat16),
        in_specs=[vmem] * 3,
        out_specs=vmem,
        scratch_shapes=[
            pltpu.VMEM((3, 4, 9, tile, tile), jnp.bfloat16),
            small,
            small,
            pltpu.VMEM(tiles, jnp.float32),
            small,
            small,
            small,
            small,
            small,
            small,
            pltpu.VMEM((2, 2, FOLD, LANES), jnp.bfloat16),
            pltpu.VMEM((2, 2, 2, FOLD, LANES), jnp.bfloat16),
            folded,
            folded,
            folded,
            folded,
            dma((2, 2)),
            dma((2, 2)),
            dma((len(SIDE),)),
            dma((len(SIDE),)),
            dma((2, len(PASS_ON))),
            dma((2, len(PASS_ON))),
            dma((remote, 2)),
            dma((remote, 2)),
            dma((remote, 2)),
            dma((remote, 2)),
        ],
        compiler_params=pltpu.CompilerParams(
            collective_id=0, has_side_effects=True, vmem_limit_bytes=56 * 2**20
        ),
        name="tangent_step",
    )(base_density, tangent_density, pattern)


def solution(mesh):
    spec = P(("groups", "row"), "col", None, None, None)
    return jax.shard_map(
        functools.partial(shards, mesh.shape["row"], mesh.shape["col"]),
        mesh=mesh,
        in_specs=(spec, spec, P("row", "col", None, None, None)),
        out_specs=spec,
        check_vma=False,
    )
```

time: 100 us -> 73.5 us (0.73)
  Pallas kernels: 95.6 us -> 68.9 us
    pallas_call x1, Pallas kernels: 95.6 us -> 68.9 us  [shards(): pl.pallas_call(functools.partial(kernel, rows, cols), out_shape=jax.Shape...]
where the time goes in v2:
time: 73.5 us; the launch traced here: 73.3 us
  Pallas kernels  68.9 us (94%)
  local copies, waits for them, and re-layouts  4.38 us (6%)
    pallas_call x1, Pallas kernels, shards(): pl.pallas_call(functools.partial(kernel, rows, cols), out_shape=jax.Shape...  68.9 us
    unnamed x2, local copies, waits for them, and re-layouts  4.38 us

profile of v2, /device:TPU:0, one launch (start us, length us, event | category | flops | bytes accessed | tf_op | source)
XLA Modules:
  0.0 73.3 jit_solution(14140628919457968558)
XLA Ops:
  0.0 1.6 %copy.4.pattern = s32[1,2,9,8,8]{4,3,2,1,0:T(8,128)} copy(s32[1,2,9,8,8]{2,4,3,1,0:T(8,128)} %param.5) | data formatting | bytes 9216 | tf_op args[2]
  1.6 68.9 %tangent_step.1 = bf16[1,2,9,184,184]{4,3,2,1,0:T(8,128)(2,1)} custom-call(bf16[1,2,9,184,184]{4,3,2,1,0:T(8,128)(2,1)} %base.1, bf16[1,2,9,184,184]{4,3,2,1,0:T(8,128)(2,1)} %tangent.1, s32[1,2,9,8,8]{4,3,2,1,0:T(8,128)} %copy.4.pattern), custom_call_target="tpu_custom_call" | custom-call | tf_op jit(solution)/shard_map/tangent_step/pallas_call | solution.py:339
  70.5 2.7 %copy.6 = bf16[1,2,9,184,184]{4,3,2,1,0:T(8,128)(2,1)} copy(bf16[1,2,9,184,184]{4,3,2,1,0:T(8,128)(2,1)} %tangent_step.1) | data formatting | bytes 2437632

commit v3 on v2

--- a/solution.py
+++ b/solution.py
@@ -33,7 +33,7 @@
     return plan
 
 
-PASS_ON = ((1, 1, 4, 2), (-1, 0, 4, 1))
+PASS_ON = ((-1, 0, 4, 1), (1, 1, 4, 2))
 LANES = 128
 FOLD = 96
 
@@ -69,7 +69,8 @@
 
 
 def kernel(
-    rows, cols, base, tangent, pattern, out,
+    rows, cols, base_far, tangent_far, pattern_far, out,
+    base, tangent, pattern, load,
     q, p, mask, r32, rb, rt, f, gt, g, s,
     own_fold, halo_fold, rt_fold, f_fold, g_fold, gt_fold,
     z_send, z_recv, h_send, h_recv, n_send, n_recv, r_send, r_recv, g_send, g_recv,
@@ -79,6 +80,15 @@
     col = lax.axis_index("col")
     tile = base.shape[-1]
 
+    loads = [
+        pltpu.make_async_copy(far, near, load.at[k])
+        for k, (far, near) in enumerate(
+            ((pattern_far, pattern), (base_far, base), (tangent_far, tangent))
+        )
+    ]
+    for copy in loads:
+        copy.start()
+
     def device(dr, dc):
         return (group, lax.rem(row + dr + rows, rows), lax.rem(col + dc + cols, cols))
 
@@ -94,6 +104,9 @@
     wide_r = lax.broadcasted_iota(jnp.int32, (blocks, tile), 0) * BLOCK
     wide_c = lax.broadcasted_iota(jnp.int32, (blocks, tile), 1)
     wide = ((wide_c >= wide_r) & (wide_c < wide_r + BLOCK)).astype(jnp.float32).astype(jnp.bfloat16)
+
+    loads[0].wait()
+    loads[1].wait()
 
     def prepare(c, o):
         pat = pattern[0, c, o].astype(jnp.float32).astype(jnp.bfloat16)
@@ -104,29 +117,22 @@
         q[1, 1 + c, o] = kept
         return kept
 
-    @pl.loop(0, 2)
-    def _(c):
-        for e in range(2):
-            fold(own_fold.at[c, e], prepare(c, 4 + e))
-
-    pl.semaphore_wait(barrier, 8)
-
-    def over_rows(k):
-        left = (pl.ds(1, 2), pl.ds(4, 2), slice(None), pl.ds(0, LANES))
+    def over_rows(k, c):
+        left = (1 + c, pl.ds(4, 2), slice(None), pl.ds(0, LANES))
         return [
             pltpu.make_async_remote_copy(
                 src_ref=q.at[(1,) + left],
                 dst_ref=q.at[(1 - STEPS[k],) + left],
-                send_sem=z_send.at[k, 0],
-                recv_sem=z_recv.at[k, 0],
+                send_sem=z_send.at[k, c, 0],
+                recv_sem=z_recv.at[k, c, 0],
                 device_id=device(STEPS[k], 0),
                 device_id_type=MESH,
             ),
             pltpu.make_async_remote_copy(
-                src_ref=own_fold,
-                dst_ref=halo_fold.at[k],
-                send_sem=z_send.at[k, 1],
-                recv_sem=z_recv.at[k, 1],
+                src_ref=own_fold.at[c],
+                dst_ref=halo_fold.at[k, c],
+                send_sem=z_send.at[k, c, 1],
+                recv_sem=z_recv.at[k, c, 1],
                 device_id=device(STEPS[k], 0),
                 device_id_type=MESH,
             ),
@@ -142,10 +148,15 @@
             device_id_type=MESH,
         )
 
-    halo = [over_rows(k) for k in range(2)]
-    for pair in halo:
-        for copy in pair:
-            copy.start()
+    halo = [[over_rows(k, c) for c in range(2)] for k in range(2)]
+    for c in range(2):
+        for e in range(2):
+            fold(own_fold.at[c, e], prepare(c, 4 + e))
+        if c == 0:
+            pl.semaphore_wait(barrier, 8)
+        for k in range(2):
+            for copy in halo[k][c]:
+                copy.start()
 
     @pl.loop(0, 2)
     def _(c):
@@ -157,6 +168,8 @@
         copy = within_row(1, dc, c, first, count, h_send.at[k], h_recv.at[k])
         copy.start()
         side.append(copy)
+
+    loads[2].wait()
 
     @pl.loop(0, 18)
     def _(i):
@@ -246,24 +259,25 @@
         def _(c):
             r32[c, o] = product(p, c, o, True)
 
+    def complete(c, o):
+        finish_r(c, o, r32[c, o] + product(p, c, o, False))
+        hand_over(back_r, rt, f, c, o)
+
     passed = []
-    for k, dr in enumerate(STEPS):
-        x = 1 - dr
-        for copy in halo[k]:
-            copy.wait_recv()
-        for c in range(2):
+    for c in range(2):
+        for k, dr in enumerate(STEPS):
+            x = 1 - dr
+            for copy in halo[k][c]:
+                copy.wait_recv()
             for e in range(2):
                 unfold(q.at[x, 1 + c, 4 + e], halo_fold.at[k, c, e])
-        for i, (dc, c, first, count) in enumerate(PASS_ON):
-            copy = within_row(x, dc, c, first, count, n_send.at[k, i], n_recv.at[k, i])
+            dc, _, first, count = PASS_ON[c]
+            copy = within_row(x, dc, c, first, count, n_send.at[k, c], n_recv.at[k, c])
             copy.start()
             passed.append(copy)
-        flip((-dr, 0), 5)
-        flip((-dr, 1), 5)
-        for c, sy in ((1, 0), (1, -1), (0, 1)):
-            o = (x * 3) + sy + 1
-            finish_r(c, o, r32[c, o] + product(p, c, o, False))
-            hand_over(back_r, rt, f, c, o)
+            flip((-dr, c), 5)
+            for own, sy in (((1, -1),), ((1, 0), (0, 1)))[c]:
+                complete(own, x * 3 + sy + 1)
 
     for copy in passed:
         copy.wait_recv()
@@ -271,9 +285,7 @@
         x = 1 - dr
         flip((-dr, -1), 5)
         for c, sy in ((0, 0), (0, -1), (1, 1)):
-            o = (x * 3) + sy + 1
-            finish_r(c, o, r32[c, o] + product(p, c, o, False))
-            hand_over(back_r, rt, f, c, o)
+            complete(c, x * 3 + sy + 1)
 
     for o in ORDER:
         @pl.loop(0, 2)
@@ -321,7 +333,7 @@
         unfold(gt.at[other, 8 - o], gt_fold.at[other, 8 - o])
         finish(other, 8 - o)
 
-    for copy in halo[0] + halo[1] + side + passed:
+    for copy in sum(halo[0] + halo[1], []) + side + passed:
         copy.wait_send()
     for c, o in REMOTE:
         for copy in back_r(c, o) + back_g(c, o):
@@ -339,9 +351,13 @@
     return pl.pallas_call(
         functools.partial(kernel, rows, cols),
         out_shape=jax.ShapeDtypeStruct(base_density.shape, jnp.bfloat16),
-        in_specs=[vmem] * 3,
+        in_specs=[pl.BlockSpec(memory_space=pl.ANY)] * 3,
         out_specs=vmem,
         scratch_shapes=[
+            pltpu.VMEM(base_density.shape, jnp.bfloat16),
+            pltpu.VMEM(base_density.shape, jnp.bfloat16),
+            pltpu.VMEM(pattern.shape, pattern.dtype),
+            dma((3,)),
             pltpu.VMEM((3, 4, 9, tile, tile), jnp.bfloat16),
             small,
             small,
@@ -358,8 +374,8 @@
             folded,
             folded,
             folded,
-            dma((2, 2)),
-            dma((2, 2)),
+            dma((2, 2, 2)),
+            dma((2, 2, 2)),
             dma((len(SIDE),)),
             dma((len(SIDE),)),
             dma((2, len(PASS_ON))),

time: 73.5 us -> 72.8 us (level)
  no operation moved by 1% of the time
where the time goes in v3:
time: 72.8 us; the launch traced here: 72.6 us
  Pallas kernels  68.2 us (94%)
  local copies, waits for them, and re-layouts  4.38 us (6%)
    pallas_call x1, Pallas kernels, shards(): pl.pallas_call(functools.partial(kernel, rows, cols), out_shape=jax.Shape...  68.2 us
    unnamed x2, local copies, waits for them, and re-layouts  4.38 us

profile of v3, /device:TPU:0, one launch (start us, length us, event | category | flops | bytes accessed | tf_op | source)
XLA Modules:
  0.0 72.6 jit_solution(13361250069284157067)
XLA Ops:
  0.0 1.6 %copy.4.pattern_far = s32[1,2,9,8,8]{4,3,2,1,0:T(8,128)} copy(s32[1,2,9,8,8]{2,4,3,1,0:T(8,128)} %param.5) | data formatting | bytes 9216 | tf_op args[2]
  1.6 68.2 %tangent_step.1 = bf16[1,2,9,184,184]{4,3,2,1,0:T(8,128)(2,1)} custom-call(bf16[1,2,9,184,184]{4,3,2,1,0:T(8,128)(2,1)} %base_far.1, bf16[1,2,9,184,184]{4,3,2,1,0:T(8,128)(2,1)} %tangent_far.1, s32[1,2,9,8,8]{4,3,2,1,0:T(8,128)} %copy.4.pattern_far), custom_call_target="tpu_custom_call" | custom-call | tf_op jit(solution)/shard_map/tangent_step/pallas_call | solution.py:351
  69.9 2.7 %copy.6 = bf16[1,2,9,184,184]{4,3,2,1,0:T(8,128)(2,1)} copy(bf16[1,2,9,184,184]{4,3,2,1,0:T(8,128)(2,1)} %tangent_step.1) | data formatting | bytes 2437632
